TPU v7x, 512 devices: a whole 4x4x16 slice. The times are simulated.
512 devices in a mesh: rep: 16 (over z_hi, y), seq: 32 (over z_lo, x, core).
Axes of the slice: x: 4, y: 4, z: 16 (z_hi: 4, z_lo: 4; z = z_hi * 4 + z_lo), core: 2. Of those that a mesh axis runs over, the one named last changes fastest.
Arguments:
- qkv_spatial: bfloat16 [131072, 1728], P(('rep', 'seq')), may hold values from -5.5 to 5.5
- qkv_temporal: bfloat16 [131072, 1728], P(('rep', 'seq')), may hold values from -5.5 to 5.5
- out_grad: bfloat16 [131072, 1152], P(('rep', 'seq')), may hold values from -6 to 6
- out_proj: bfloat16 [576, 2, 1152], P('seq'), may hold values from -0.25 to 0.25
Outputs:
- qkv_spatial_grad: bfloat16 [131072, 1728], P(('rep', 'seq'))
- qkv_temporal_grad: bfloat16 [131072, 1728], P(('rep', 'seq'))
- out_proj_grad: bfloat16 [576, 2, 1152], P('seq')
All inputs are finite; a program needn't handle non-finite values.
Results may differ from a plain program's by a relative error of at most 0.015.
Values may be sent and summed in bfloat16 or wider, within the bound.
A program may use at most 128 MiB of HBM per device.

v0:
```python
import jax
import jax.numpy as jnp
from jax import lax
from jax.sharding import PartitionSpec as P

HEADS = 8
HEAD_DIM = 72
PATCHES = 256


def product(layout, left, right):
    return jnp.einsum(layout, left, right, preferred_element_type=jnp.float32)


def attend(query, keys, values, layout):
    key_layout = layout.replace("l", "m")
    scaling = query.shape[-1] ** (-0.5)
    scores = product(layout + "," + key_layout + "->ghlm", query, keys) * scaling
    highest = jnp.max(scores, axis=-1, keepdims=True)
    weights = jnp.exp(scores - highest)
    probs = weights / jnp.sum(weights, axis=-1, keepdims=True)
    mixed = product(
        "ghlm," + key_layout + "->" + layout, probs.astype(jnp.bfloat16), values
    ).astype(jnp.bfloat16)
    return (mixed, probs)


def attend_back(query, keys, values, probs, grad_mixed, layout):
    key_layout = layout.replace("l", "m")
    scaling = query.shape[-1] ** (-0.5)
    rounded = probs.astype(jnp.bfloat16)
    grad_values = product("ghlm," + layout + "->" + key_layout, rounded, grad_mixed)
    grad_probs = product(layout + "," + key_layout + "->ghlm", grad_mixed, values)
    grad_scores = (
        probs * (grad_probs - jnp.sum(grad_probs * probs, axis=-1, keepdims=True))
    ).astype(jnp.bfloat16)
    grad_query = product("ghlm," + key_layout + "->" + layout, grad_scores, keys) * scaling
    grad_keys = product("ghlm," + layout + "->" + key_layout, grad_scores, query) * scaling
    return (grad_query, grad_keys, grad_values)


def per_device(qkv_spatial, qkv_temporal, out_grad, out_proj):
    seq_count = lax.axis_size("seq")
    rep_count = lax.axis_size("rep")
    row_count = qkv_spatial.shape[0]
    frames_dev = row_count // PATCHES
    inner_width = HEADS * HEAD_DIM
    factor = float(row_count * seq_count * rep_count) ** (-0.5)
    spatial = qkv_spatial.reshape(frames_dev, PATCHES, 3, HEADS, HEAD_DIM)
    spatial_mixed, spatial_probs = attend(
        spatial[:, :, 0], spatial[:, :, 1], spatial[:, :, 2], "glhe"
    )
    spatial_flat = spatial_mixed.reshape(row_count, inner_width)
    local_fields = qkv_temporal.reshape(frames_dev, PATCHES, 3 * inner_width)
    patch_fields = lax.all_to_all(local_fields, "seq", split_axis=1, concat_axis=0, tiled=True)
    frames_all = patch_fields.shape[0]
    patch_dev = patch_fields.shape[1]
    temporal = patch_fields.reshape(frames_all, patch_dev, 3, HEADS, HEAD_DIM)
    temporal_mixed, temporal_probs = attend(
        temporal[:, :, 0], temporal[:, :, 1], temporal[:, :, 2], "lghe"
    )
    returned = lax.all_to_all(
        temporal_mixed.reshape(frames_all, patch_dev, inner_width),
        "seq",
        split_axis=0,
        concat_axis=1,
        tiled=True,
    )
    temporal_rows = returned.reshape(row_count, inner_width)
    block_rows = lax.all_gather(out_proj, "seq", axis=0, tiled=True)
    spatial_part = product("td,nd->tn", out_grad, block_rows[:, 0])
    temporal_part = product("td,nd->tn", out_grad, block_rows[:, 1])
    grad_mixed = jnp.stack([spatial_part, temporal_part], axis=1).astype(jnp.bfloat16)
    spatial_grad = grad_mixed[:, 0].reshape(frames_dev, PATCHES, HEADS, HEAD_DIM)
    spatial_back = attend_back(
        spatial[:, :, 0], spatial[:, :, 1], spatial[:, :, 2], spatial_probs, spatial_grad, "glhe"
    )
    spatial_fields = (
        jnp.stack(spatial_back, axis=2).astype(jnp.bfloat16).reshape(row_count, 3 * inner_width)
    )
    grad_local = grad_mixed[:, 1].reshape(frames_dev, PATCHES, inner_width)
    grad_patch = lax.all_to_all(grad_local, "seq", split_axis=1, concat_axis=0, tiled=True)
    temporal_grad = grad_patch.reshape(frames_all, patch_dev, HEADS, HEAD_DIM)
    temporal_back = attend_back(
        temporal[:, :, 0],
        temporal[:, :, 1],
        temporal[:, :, 2],
        temporal_probs,
        temporal_grad,
        "lghe",
    )
    temporal_stack = (
        jnp.stack(temporal_back, axis=2)
        .astype(jnp.bfloat16)
        .reshape(frames_all, patch_dev, 3 * inner_width)
    )
    temporal_fields = lax.all_to_all(
        temporal_stack, "seq", split_axis=0, concat_axis=1, tiled=True
    ).reshape(row_count, 3 * inner_width)
    columns = spatial_flat
    spatial_share = lax.psum_scatter(
        product("tn,td->nd", columns, out_grad) * factor, "seq", scatter_dimension=0, tiled=True
    )
    columns = temporal_rows
    temporal_share = lax.psum_scatter(
        product("tn,td->nd", columns, out_grad) * factor, "seq", scatter_dimension=0, tiled=True
    )
    shares = jnp.stack([spatial_share, temporal_share], axis=1)
    summed = lax.psum(shares, "rep")
    return (spatial_fields, temporal_fields, summed.astype(jnp.bfloat16))


def solution(mesh):
    placed = (
        P(("rep", "seq"), None),
        P(("rep", "seq"), None),
        P(("rep", "seq"), None),
        P("seq", None, None),
    )
    return jax.shard_map(
        per_device,
        mesh=mesh,
        in_specs=placed,
        out_specs=(P(("rep", "seq"), None), P(("rep", "seq"), None), P("seq", None, None)),
        check_vma=False,
    )
```

profile of v0, /device:TPU:2, one launch (start us, length us, event | category | flops | bytes accessed | tf_op | source)
XLA Modules:
  0.0 528.8 jit_solution(12527915253286516009)
XLA Ops:
  7.2 0.7 all-gather.2.cloned.1.call-update
  7.9 3.9 copy.57
  11.8 0.5 broadcast.47
  12.3 6.5 %reduce.11 = bf16[256,1728]{1,0:T(8,128)(2,1)S(1)} reduce(bf16[256,1,1728]{2,1,0:T(2,128)(2,1)S(1)} %bitcast.147, bf16[]{:T(256)} %broadcast.47), dimensions={1}, to_apply=%bitcast.120.reduce_sub_computation | reduce | bytes 1769474
  18.8 1.8 reshape.161
  20.7 9.5 %all-to-all-start = ((bf16[32,2,6912]{2,1,0:T(2,128)(2,1)}), bf16[32,2,6912]{2,1,0:T(2,128)(2,1)S(1)}, u32[]{:S(2)}, u32[]{:S(2)}) async-start(bf16[32,2,6912]{2,1,0:T(2,128)(2,1)} %reshape.161), calls=%async_computation | async-start | bytes 1769472 | tf_op jit(solution)/shard_map/all_to_all | solution.py:55
  30.2 2.2 fusion.37
  32.3 26.1 %all-to-all-done = bf16[32,2,6912]{2,1,0:T(2,128)(2,1)S(1)} async-done(((bf16[32,2,6912]{2,1,0:T(2,128)(2,1)}), bf16[32,2,6912]{2,1,0:T(2,128)(2,1)S(1)}, u32[]{:S(2)}, u32[]{:S(2)}) %all-to-all-start) | async-done | bytes 884768 | tf_op jit(solution)/shard_map/all_to_all | solution.py:55
  58.5 1.5 reshape.162
  60.0 5.1 bitcast_reduce_fusion
  65.2 1.8 reshape.149
  66.9 1.3 fusion.36
  68.2 1.0 fusion.38
  69.2 1.0 copy-done.7
  70.1 1.6 fusion.12
  71.9 1.1 reshape.153
  73.0 5.2 all-to-all-start.3
  78.2 8.3 %all-gather.2.cloned.1.call-done = bf16[576,2,1152]{2,1,0:T(2,128)(2,1)} async-done(((bf16[18,2,1152]{2,1,0:T(2,128)(2,1)}), bf16[576,2,1152]{2,1,0:T(2,128)(2,1)}) %all-gather.2.cloned.1.call-update) | async-done | bytes 2654224 | tf_op jit(solution)/shard_map/all_gather | solution.py:70
  86.5 7.9 %fusion.35 = (bf16[576,1,1152]{2,1,0:T(2,128)(2,1)S(1)}, bf16[576,1,1152]{2,1,0:T(2,128)(2,1)}) fusion(bf16[576,2,1152]{2,1,0:T(2,128)(2,1)} %all-gather.2.cloned.1.call-done), kind=kLoop, calls=%fused_computation.67 | loop fusion | bytes 5308416 | tf_op jit(solution)/shard_map/slice | solution.py:72
  94.4 1.3 fusion.18
  95.7 1.6 copy.61
  97.2 3.4 reduce.10
  100.7 2.0 reshape.159
  102.7 6.8 %all-to-all-start.1 = ((bf16[32,2,2304]{2,1,0:T(2,128)(2,1)}), bf16[32,2,2304]{2,1,0:T(2,128)(2,1)}, u32[]{:S(2)}, u32[]{:S(2)}) async-start(bf16[32,2,2304]{2,1,0:T(2,128)(2,1)} %reshape.159), calls=%async_computation.1 | async-start | bytes 589824 | tf_op jit(solution)/shard_map/all_to_all | solution.py:82
  109.8 1.3 convolution_convert_fusion.2
  111.1 2.1 convolution_multiply_fusion.1
  113.1 3.1 convolution_multiply_fusion
  116.3 3.3 all-to-all-done.1
  119.6 2.5 reshape.160
  122.1 1.8 bitcast_reduce_fusion.1
  124.0 0.6 reshape.150
  124.6 0.9 multiply_reduce_fusion.2
  125.8 0.7 copy-done.6
  126.5 0.5 fusion.10
  128.3 0.6 copy.66
  128.9 1.9 convert_element_type.55
  130.8 5.8 %all-to-all-start.2 = ((bf16[32,8,1728]{2,1,0:T(8,128)(2,1)}), bf16[32,8,1728]{2,1,0:T(8,128)(2,1)S(1)}, u32[]{:S(2)}, u32[]{:S(2)}) async-start(bf16[32,8,1728]{2,1,0:T(8,128)(2,1)} %convert_element_type.55), calls=%async_computation.2 | async-start | bytes 1835008 | tf_op jit(solution)/shard_map/all_to_all | solution.py:97
  136.6 1.3 dynamic-slice
  138.5 2.5 fusion.15
  141.0 0.5 multiply_reduce_fusion
  142.7 0.5 fusion.17
  143.2 1.0 pad_maximum_fusion.1
  144.2 17.1 %all-to-all-done.2 = bf16[32,8,1728]{2,1,0:T(8,128)(2,1)S(1)} async-done(((bf16[32,8,1728]{2,1,0:T(8,128)(2,1)}), bf16[32,8,1728]{2,1,0:T(8,128)(2,1)S(1)}, u32[]{:S(2)}, u32[]{:S(2)}) %all-to-all-start.2) | async-done | bytes 884768 | tf_op jit(solution)/shard_map/all_to_all | solution.py:97
  161.3 1.3 copy.70
  162.5 255.8 %all-reduce.6.cloned.1.call-done = (f32[576,1152]{1,0:T(8,128)}, f32[576,1152]{1,0:T(8,128)}) async-done(((f32[576,1152]{1,0:T(8,128)}, f32[576,1152]{1,0:T(8,128)}), (f32[576,1152]{1,0:T(8,128)}, f32[576,1152]{1,0:T(8,128)})) %all-reduce.6.cloned.1.call-update) | async-done | bytes 5308432
  418.3 1.0 dynamic-slice_bitcast_fusion
  419.3 101.9 %all-reduce.7 = bf16[18,2,1152]{2,0,1:T(8,128)(2,1)S(1)} all-reduce(f32[18,2,1152]{2,0,1:T(8,128)S(1)} %pad_maximum_fusion.2), channel_id=1, replica_groups=mesh['rep'=16,'seq'=32] {'rep'}, use_global_device_ids=true, to_apply=%region_8.0 | all-reduce | flops 41472 | bytes 248832 | tf_op jit(solution)/shard_map/psum | solution.py:109
  521.3 0.7 copy.71
  (35 shorter events, 3.4 us)
Async XLA Ops:
  7.2 87.2 %copy-start = (bf16[256,1152]{1,0:T(8,128)(2,1)S(1)}, bf16[256,1152]{1,0:T(8,128)(2,1)}, u32[]{:S(2)}) copy-start(bf16[256,1152]{1,0:T(8,128)(2,1)} %param.6) | copy-start | bytes 1769476
  7.2 79.3 %all-gather.2.cloned.1.call-start = ((), (), s32[]{:S(2)}) async-start(), calls=%async_computation.4 | async-start | bytes 2737152 | tf_op jit(solution)/shard_map/all_gather | solution.py:70
  18.8 11.4 %copy-start.10 = (bf16[256,1728]{0,1:T(8,128)(2,1)S(1)}, bf16[256,1728]{0,1:T(8,128)(2,1)}, u32[]{:S(2)}) copy-start(bf16[256,1728]{0,1:T(8,128)(2,1)} %param.4) | copy-start | bytes 2654212
  20.7 37.8 %all-to-all-start = ((bf16[32,2,6912]{2,1,0:T(2,128)(2,1)}), bf16[32,2,6912]{2,1,0:T(2,128)(2,1)S(1)}, u32[]{:S(2)}, u32[]{:S(2)}) async-start(bf16[32,2,6912]{2,1,0:T(2,128)(2,1)} %reshape.161), calls=%async_computation | async-start | bytes 1769472 | tf_op jit(solution)/shard_map/all_to_all | solution.py:55
  68.2 3.5 copy-start.3
  68.2 3.5 copy-start.5
  69.1 1.0 copy-start.7
  73.0 29.7 %all-to-all-start.3 = ((bf16[32,8,576]{2,1,0:T(8,128)(2,1)}), bf16[32,8,576]{2,1,0:T(8,128)(2,1)}, u32[]{:S(2)}, u32[]{:S(2)}) async-start(bf16[32,8,576]{2,1,0:T(8,128)(2,1)} %reshape.153), calls=%async_computation.3 | async-start | bytes 655360 | tf_op jit(solution)/shard_map/all_to_all | solution.py:62
  95.7 14.1 %copy-start.1 = (f32[8,256,256]{1,2,0:T(8,128)S(1)}, f32[8,256,256]{1,2,0:T(8,128)}, u32[]{:S(2)}) copy-start(f32[8,256,256]{1,2,0:T(8,128)} %get-tuple-element.23) | copy-start | bytes 6291460
  102.7 16.9 %all-to-all-start.1 = ((bf16[32,2,2304]{2,1,0:T(2,128)(2,1)}), bf16[32,2,2304]{2,1,0:T(2,128)(2,1)}, u32[]{:S(2)}, u32[]{:S(2)}) async-start(bf16[32,2,2304]{2,1,0:T(2,128)(2,1)} %reshape.159), calls=%async_computation.1 | async-start | bytes 589824 | tf_op jit(solution)/shard_map/all_to_all | solution.py:82
  109.5 308.8 %all-reduce.6.cloned.1.call-start = ((), (), s32[]{:S(2)}) async-start(), calls=%async_computation.5 | async-start | bytes 10616832
  116.2 8.3 %copy-start.8 = (f32[8,8,32,32]{2,3,1,0:T(8,128)S(1)}, f32[8,8,32,32]{2,3,1,0:T(8,128)}, u32[]{:S(2)}) copy-start(f32[8,8,32,32]{2,3,1,0:T(8,128)} %copy-done.7) | copy-start | bytes 786436
  116.3 8.3 %copy-start.9 = (bf16[32,8,1,8,72]{4,3,2,1,0:T(8,128)(2,1)S(1)}, bf16[32,8,1,8,72]{4,3,2,1,0:T(8,128)(2,1)}, u32[]{:S(2)}) copy-start(bf16[32,8,1,8,72]{4,3,2,1,0:T(8,128)(2,1)} %get-tuple-element.19) | copy-start | bytes 884740
  125.4 1.0 copy-start.6
  125.4 1.6 copy-start.4
  130.8 10.2 %copy-start.11 = (bf16[256,1728]{0,1:T(8,128)(2,1)S(1)}, bf16[256,1728]{0,1:T(8,128)(2,1)}, u32[]{:S(2)}) copy-start(bf16[256,1728]{0,1:T(8,128)(2,1)} %param.4) | copy-start | bytes 2654212
  130.8 30.5 %all-to-all-start.2 = ((bf16[32,8,1728]{2,1,0:T(8,128)(2,1)}), bf16[32,8,1728]{2,1,0:T(8,128)(2,1)S(1)}, u32[]{:S(2)}, u32[]{:S(2)}) async-start(bf16[32,8,1728]{2,1,0:T(8,128)(2,1)} %convert_element_type.55), calls=%async_computation.2 | async-start | bytes 1835008 | tf_op jit(solution)/shard_map/all_to_all | solution.py:97
  138.5 2.5 copy-start.2
Sparse Core Ops, SparseCore 0:
  10.2 76.2 all-gather.1
  116.4 301.8 all-reduce.5
where the time goes:
time: 530 us; the launch traced here: 529 us
  waiting for transfers between devices  311 us (59%)
  blocking collectives  102 us (19%)
  local copies, waits for them, and re-layouts  42.1 us (8%)
  starting transfers between devices  27.5 us (5%)
  matrix products  18.9 us (4%)
  between operations  15 us (3%)
  other arithmetic  12 us (2%)
    unnamed x3, waiting for transfers between devices  256 us
    psum x1, blocking collectives, per_device(): summed = lax.psum(shares, 'rep')  102 us
    all_to_all x1, waiting for transfers between devices, per_device(): lax.all_to_all(local_fields, 'seq', split_axis=1, concat_axis=0, tiled=True)  26.1 us
    all_to_all x1, waiting for transfers between devices, per_device(): lax.all_to_all(temporal_stack, 'seq', split_axis=0, concat_axis=1, tiled=...  17.1 us
    dot_general x14, matrix products, product(): return jnp.einsum(layout, left, right, preferred_element_type=jnp.float32)  15.8 us
    unnamed x32, local copies, waits for them, and re-layouts  13.4 us
  transfers between devices with their start and end apart: 6, of which 5 were waited for; matrix products, arithmetic and copies ran while one was open for 13% of the time, Pallas kernels for 0%

commit v1 on v0

v1 whole, which is shorter than its diff:
```python
import functools

import jax
import jax.numpy as jnp
from jax import lax
from jax.experimental import pallas as pl
from jax.experimental.pallas import tpu as pltpu
from jax.sharding import PartitionSpec as P

HEADS, HEAD_DIM, PATCHES, FRAMES = 8, 72, 256, 32
INNER, WIDTH, D = 576, 1728, 1152
PAD = 640
GROUP = 8
ROWS = 18
BLOCK = 24
HALF = 16 * BLOCK
SEQ, TOKENS = 32, 131072
SCALING = HEAD_DIM**-0.5
FACTOR = float(TOKENS) ** -0.5
F32, BF16 = jnp.float32, jnp.bfloat16


def dot(left, right, dims=((1,), (0,))):
    return lax.dot_general(left, right, (dims, ((), ())), preferred_element_type=F32)


def kernel(
    qkvs_ref, qkvt_ref, og_ref, w_ref,
    gs_ref, gt_ref, gw_ref,
    qkvs, og2, qtr, das, dar, mts, mtr, gts, wbuf, wf, wmat, sel, self32, dah, dax, m2, mx,
    gbuf, yrecv, xbuf, xrecv, zbuf, zrecv, z2buf, z2recv, res,
    qs, ks, vs, ds, qt, kt, vt, dt, probs_s, probs_t, acc0, acc1, acc2, gstage,
    lsem, wz_s, wz_r, wx_s, wx_r, og_s, og_r, a_s, a_r, b_s, b_r, c_s, c_r, d_s, d_r,
    p_s, p_r, y_s, y_r, x_s, x_r, z_s, z_r, zz_s, zz_r, f_s, f_r,
):
    rep, me = lax.axis_index("rep"), lax.axis_index("seq")
    zh, y = rep // 4, lax.rem(rep, 4)
    zl, x, core = me // 8, lax.rem(me // 2, 4), lax.rem(me, 2)
    z = 4 * zh + zl

    def at(rep_to, seq_to):
        return {"device_id": (rep_to, seq_to), "device_id_type": pl.DeviceIdType.MESH}

    def at_z(step):
        to = lax.rem(z + step + 16, 16)
        return at((to // 4) * 4 + y, lax.rem(to, 4) * 8 + lax.rem(me, 8))

    def at_y(step):
        return at(zh * 4 + lax.rem(y + step, 4), me)

    def at_zh(step):
        return at(lax.rem(zh + step, 4) * 4 + y, me)

    def at_x(step):
        return at(rep, zl * 8 + lax.rem(x + step, 4) * 2 + core)

    partner = at(rep, me + 1 - 2 * core)

    def remote(src, dst, send, recv, target):
        return pltpu.make_async_remote_copy(
            src_ref=src, dst_ref=dst, send_sem=send, recv_sem=recv, **target
        )

    barrier = pltpu.get_barrier_semaphore()

    def greet(k, carry):
        pl.semaphore_signal(barrier, inc=1, **at(rep, lax.rem(me + k, SEQ)))
        return carry

    lax.fori_loop(1, SEQ, greet, 0)
    for step in (-1, -2, 1):
        pl.semaphore_signal(barrier, inc=1, **at_z(step))
    for step in (1, 2, 3):
        pl.semaphore_signal(barrier, inc=1, **at_y(step))
        pl.semaphore_signal(barrier, inc=1, **at_zh(step))

    local = [
        pltpu.make_async_copy(qkvs_ref, qkvs, lsem.at[0]),
        pltpu.make_async_copy(og_ref, og2.at[pl.ds(0, PATCHES)], lsem.at[1]),
        pltpu.make_async_copy(qkvt_ref.at[me], qtr.at[me], lsem.at[2]),
        pltpu.make_async_copy(w_ref.at[0], wbuf.at[0, x, zl], lsem.at[3]),
        pltpu.make_async_copy(w_ref.at[1], wbuf.at[1, x, zl], lsem.at[4]),
    ]
    for copy in local:
        copy.start()

    pl.semaphore_wait(barrier, 31 + 9)

    wz = [
        [
            remote(w_ref.at[b], wbuf.at[b, x, zl], wz_s.at[b, i], wz_r.at[b, i], at_z(step))
            for i, step in enumerate((1, 2, -1))
        ]
        for b in (0, 1)
    ]
    for copy in wz[1] + wz[0]:
        copy.start()
    og_copy = remote(
        og_ref, og2.at[pl.ds(PATCHES, PATCHES)], og_s.at[0], og_r.at[0], partner
    )
    og_copy.start()

    def exchange(src, dst, send, recv):
        def copy(k):
            to = lax.rem(me + k, SEQ)
            return remote(src.at[to], dst.at[me], send.at[k], recv.at[k], at(rep, to))

        def start(k, carry):
            copy(k).start()
            return carry

        def landed(k, carry):
            copy(k).wait_recv()
            return carry

        def sent(k, carry):
            copy(k).wait_send()
            return carry

        return (
            lambda: lax.fori_loop(1, SEQ, start, 0),
            lambda: lax.fori_loop(1, SEQ, landed, 0),
            lambda: lax.fori_loop(1, SEQ, sent, 0),
        )

    fields_out = exchange(qkvt_ref, qtr, a_s, a_r)
    grads_out = exchange(das, dar, b_s, b_r)
    mixed_back = exchange(mts, mtr, c_s, c_r)
    fields_back = exchange(gts, gt_ref, d_s, d_r)
    fields_out[0]()

    def fill_sel(i, carry):
        xx, zz = i // 4, lax.rem(i, 4)
        j = lax.broadcasted_iota(jnp.int32, (BLOCK, PAD), 0)
        n = lax.broadcasted_iota(jnp.int32, (BLOCK, PAD), 1)
        rows = pl.ds(pl.multiple_of(i * BLOCK, BLOCK), BLOCK)
        for which in (0, 1):
            parity = core if which == 0 else 1 - core
            first = ROWS * (8 * zz + 2 * xx + parity)
            hit = (n == first + j) & (j < ROWS)
            self32[which, rows, :] = jnp.where(hit, 1.0, 0.0)
        return carry

    lax.fori_loop(0, 16, fill_sel, 0)
    for which in (0, 1):
        sel[which] = self32[which].astype(BF16)
    wf[...] = jnp.zeros_like(wf)

    def split(fields, q, k, v):
        q[...] = fields[:, 0:PAD].astype(BF16)
        k[...] = pltpu.roll(fields[:, 512:1152], PAD - 64, 1).astype(BF16)
        v[:, 512:PAD] = jnp.zeros((PATCHES, PAD - 512), BF16)
        v[:, 0:INNER] = fields[:, 1152:WIDTH].astype(BF16)

    def window(h):
        first = (HEAD_DIM * h) // 128
        lane = lax.broadcasted_iota(jnp.int32, (1, 256), 1) + first * 128 - HEAD_DIM * h
        keep = jnp.where((lane >= 0) & (lane < HEAD_DIM), 1.0, 0.0).astype(BF16)
        return pl.ds(pl.multiple_of(first * 128, 128), 256), keep

    def forward(q, k, v, probs, mixed, same_patch):
        mixed[...] = jnp.zeros_like(mixed)

        def head(h, carry):
            cols, keep = window(h)
            scores = dot(q[:, cols], k[:, cols] * keep, ((1,), (1,))) * SCALING
            if same_patch:
                a = lax.broadcasted_iota(jnp.int32, scores.shape, 0)
                b = lax.broadcasted_iota(jnp.int32, scores.shape, 1)
                scores = jnp.where(((a ^ b) & (GROUP - 1)) == 0, scores, -1e30)
            weights = jnp.exp(scores - jnp.max(scores, axis=1, keepdims=True))
            p = weights / jnp.sum(weights, axis=1, keepdims=True)
            probs[h] = p
            mixed[:, cols] += dot(p.astype(BF16), v[:, cols] * keep)
            return carry

        lax.fori_loop(0, HEADS, head, 0)

    def backward(q, k, v, dm, probs, dq, dk, dv):
        for out in (dq, dk, dv):
            out[...] = jnp.zeros_like(out)

        def head(h, carry):
            cols, keep = window(h)
            p = probs[h]
            dm_h = dm[:, cols] * keep
            dv[:, cols] += dot(p.astype(BF16), dm_h, ((0,), (0,)))
            dp = dot(dm_h, v[:, cols], ((1,), (1,)))
            dsc = (p * (dp - jnp.sum(dp * p, axis=1, keepdims=True))).astype(BF16)
            dq[:, cols] += dot(dsc, k[:, cols] * keep)
            dk[:, cols] += dot(dsc, q[:, cols] * keep, ((0,), (0,)))
            return carry

        lax.fori_loop(0, HEADS, head, 0)

    def joined(dq, dk, dv, store):
        a = dq[...] * SCALING
        b = pltpu.roll(dk[...] * SCALING, 64, 1)
        store(0, 512, a[:, 0:512])
        store(512, 640, a[:, 512:PAD] + b[:, 0:128])
        store(640, 1152, b[:, 128:PAD])
        store(1152, WIDTH, dv[:, 0:INNER])

    local[0].wait()
    split(qkvs[...].astype(F32), qs, ks, vs)
    forward(qs, ks, vs, probs_s, acc0, False)

    def rows_x(b):
        return [
            remote(
                wbuf.at[b, x], wbuf.at[b, x], wx_s.at[b, step], wx_r.at[b, step], at_x(step)
            )
            for step in (1, 2, 3)
        ]

    wx = [rows_x(b) for b in (0, 1)]
    for b in (1, 0):
        local[3 + b].wait()
        for copy in wz[b]:
            copy.wait_recv()
        for copy in wx[b]:
            copy.start()

    def mixed_start(b, mixed):
        m2[b, 0:PATCHES, :] = dot(mixed, sel[0], ((1,), (1,))).astype(BF16)
        mx[b] = dot(mixed, sel[1], ((1,), (1,))).astype(BF16)
        copy = remote(
            mx.at[b], m2.at[b, pl.ds(PATCHES, PATCHES)], p_s.at[b], p_r.at[b], partner
        )
        copy.start()
        return copy

    def reduce_y_start(b):
        gstage[...] = dot(m2[b], og2[...], ((0,), (0,))) * FACTOR

        def put(i, carry):
            rows = pl.ds(pl.multiple_of(i * BLOCK, BLOCK), BLOCK)
            gbuf[b, lax.rem(i, 4), i // 4] = gstage[rows, :][0:ROWS].astype(BF16)
            return carry

        lax.fori_loop(0, 16, put, 0)
        copies = [
            remote(
                gbuf.at[b, lax.rem(y + step, 4)], yrecv.at[b, step],
                y_s.at[b, step], y_r.at[b, step], at_y(step),
            )
            for step in (1, 2, 3)
        ]
        for copy in copies:
            copy.start()
        return copies

    def reduce_x_start(b, copies):
        for copy in copies:
            copy.wait()
        for i in range(4):
            total = gbuf[b, y, i].astype(F32)
            for step in (1, 2, 3):
                total += yrecv[b, step, i].astype(F32)
            xbuf[b, i] = total.astype(BF16)
        copies = [
            remote(
                xbuf.at[b, lax.rem(x + step, 4)], xrecv.at[b, step],
                x_s.at[b, step], x_r.at[b, step], at_x(step),
            )
            for step in (1, 2, 3)
        ]
        for copy in copies:
            copy.start()
        return copies

    def reduce_z_start(b, copies):
        for copy in copies:
            copy.wait()
        total = xbuf[b, x].astype(F32)
        for step in (1, 2, 3):
            total += xrecv[b, step].astype(F32)
        zbuf[b] = total.astype(BF16)

        @pl.when(zl != y)
        def _():
            gather_z(b, 0).start()

    def gather_z(b, step):
        slot = lax.rem(zl - y + 4, 4) if step == 0 else step
        return remote(
            zbuf.at[b], zrecv.at[b, slot], z_s.at[b], z_r.at[b, slot],
            at(rep, y * 8 + lax.rem(me, 8)),
        )

    def spread_zh(b):
        return [
            remote(
                z2buf.at[b], z2recv.at[b, step], zz_s.at[b, step], zz_r.at[b, step], at_zh(step)
            )
            for step in (1, 2, 3)
        ]

    def reduce_zh_start(b):
        @pl.when(zl != y)
        def _():
            gather_z(b, 0).wait_send()

        @pl.when(zl == y)
        def _():
            total = zbuf[b].astype(F32)
            for step in (1, 2, 3):
                gather_z(b, step).wait_recv()
                total += zrecv[b, step].astype(F32)
            z2buf[b] = total.astype(BF16)
            for copy in spread_zh(b):
                copy.start()

    def spread_y(b):
        return [
            remote(res.at[b], res.at[b], f_s.at[b, step], f_r.at[b], at_y(step))
            for step in (1, 2, 3)
        ]

    def spread_start(b):
        @pl.when(zl == y)
        def _():
            total = z2buf[b].astype(F32)
            for step, copy in zip((1, 2, 3), spread_zh(b), strict=True):
                copy.wait()
                total += z2recv[b, step].astype(F32)
            res[b] = total.astype(BF16)
            for copy in spread_y(b):
                copy.start()

    def spread_end(b):
        @pl.when(zl == y)
        def _():
            for copy in spread_y(b):
                copy.wait_send()

        @pl.when(zl != y)
        def _():
            spread_y(b)[0].wait_recv()

    mixed_s = mixed_start(0, acc0[...].astype(BF16))

    def grad_mixed(b):
        for copy in wx[b]:
            copy.wait_recv()

        def put(i, carry):
            rows = pl.ds(pl.multiple_of(i * BLOCK, BLOCK), BLOCK)
            block = wbuf[b, i // 4, lax.rem(i, 4)].astype(F32)
            wf[rows, :] = jnp.concatenate([block, jnp.zeros((BLOCK - ROWS, D), F32)], axis=0)
            return carry

        lax.fori_loop(0, 16, put, 0)
        wmat[...] = wf[...].astype(BF16)
        dah[b] = dot(og2[...], wmat[...], ((1,), (1,))).astype(BF16)
        copy = remote(
            dah.at[b, pl.ds(PATCHES, PATCHES)], dax.at[b], p_s.at[2 + b], p_r.at[2 + b], partner
        )
        copy.start()
        mine = dot(dah[b, 0:PATCHES, :], sel[0])
        copy.wait()
        return mine + dot(dax[b], sel[1])

    local[1].wait()
    og_copy.wait()
    dmt = grad_mixed(1)
    das[...] = dmt[:, 0:INNER].reshape(FRAMES, GROUP, INNER).astype(BF16)
    grads_out[0]()
    own = [
        pltpu.make_async_copy(das.at[me], dar.at[me], lsem.at[5]),
        pltpu.make_async_copy(mts.at[me], mtr.at[me], lsem.at[6]),
        pltpu.make_async_copy(gts.at[me], gt_ref.at[me], lsem.at[7]),
        pltpu.make_async_copy(res, gw_ref, lsem.at[8]),
        pltpu.make_async_copy(qkvs, gs_ref, lsem.at[9]),
    ]
    own[0].start()

    mixed_s.wait()
    share_s = reduce_y_start(0)

    local[2].wait()
    fields_out[1]()
    split(qtr[...].astype(F32).reshape(PATCHES, WIDTH), qt, kt, vt)
    forward(qt, kt, vt, probs_t, acc0, True)
    mts[...] = acc0[:, 0:INNER].reshape(FRAMES, GROUP, INNER).astype(BF16)
    mixed_back[0]()
    own[1].start()

    share_s = reduce_x_start(0, share_s)

    own[0].wait()
    grads_out[1]()
    dt[:, 512:PAD] = jnp.zeros((PATCHES, PAD - 512), BF16)
    dt[:, 0:INNER] = dar[...].astype(F32).reshape(PATCHES, INNER).astype(BF16)
    backward(qt, kt, vt, dt, probs_t, acc0, acc1, acc2)

    def put_temporal(low, high, value):
        gts[:, :, low:high] = value.reshape(FRAMES, GROUP, high - low).astype(BF16)

    joined(acc0, acc1, acc2, put_temporal)
    fields_back[0]()
    own[2].start()

    reduce_z_start(0, share_s)

    own[1].wait()
    mixed_back[1]()
    mixed_t = mixed_start(1, jnp.concatenate(
        [mtr[...].astype(F32).reshape(PATCHES, INNER), jnp.zeros((PATCHES, PAD - INNER), F32)], axis=1
    ).astype(BF16))
    mixed_t.wait()
    share_t = reduce_y_start(1)
    reduce_zh_start(0)

    dms = grad_mixed(0)
    ds[...] = dms.astype(BF16)
    spread_start(0)
    share_t = reduce_x_start(1, share_t)
    backward(qs, ks, vs, ds, probs_s, acc0, acc1, acc2)

    def put_spatial(low, high, value):
        qkvs[:, low:high] = value.astype(BF16)

    joined(acc0, acc1, acc2, put_spatial)
    own[4].start()

    reduce_z_start(1, share_t)
    reduce_zh_start(1)
    spread_start(1)
    spread_end(0)
    spread_end(1)
    own[3].start()

    for copy in [c for b in (0, 1) for c in wz[b] + wx[b]]:
        copy.wait_send()
    fields_out[2]()
    grads_out[2]()
    mixed_back[2]()
    fields_back[1]()
    fields_back[2]()
    for copy in own[2:]:
        copy.wait()


def per_device(qkv_spatial, qkv_temporal, out_grad, out_proj):
    def vmem(*shape, dtype=BF16):
        return pltpu.VMEM(shape, dtype)

    dma = pltpu.SemaphoreType.DMA
    scratch = [
        vmem(PATCHES, WIDTH),
        vmem(2 * PATCHES, D),
        vmem(FRAMES, GROUP, WIDTH),
        vmem(FRAMES, GROUP, INNER),
        vmem(FRAMES, GROUP, INNER),
        vmem(FRAMES, GROUP, INNER),
        vmem(FRAMES, GROUP, INNER),
        vmem(FRAMES, GROUP, WIDTH),
        vmem(2, 4, 4, ROWS, D),
        vmem(HALF, D, dtype=F32),
        vmem(HALF, D),
        vmem(2, HALF, PAD),
        vmem(2, HALF, PAD, dtype=F32),
        vmem(2, 2 * PATCHES, HALF),
        vmem(2, PATCHES, HALF),
        vmem(2, 2 * PATCHES, HALF),
        vmem(2, PATCHES, HALF),
        vmem(2, 4, 4, ROWS, D),
        vmem(2, 4, 4, ROWS, D),
        vmem(2, 4, ROWS, D),
        vmem(2, 4, ROWS, D),
        vmem(2, ROWS, D),
        vmem(2, 4, ROWS, D),
        vmem(2, ROWS, D),
        vmem(2, 4, ROWS, D),
        vmem(2, ROWS, D),
        *[vmem(PATCHES, PAD) for _ in range(8)],
        vmem(HEADS, PATCHES, PATCHES, dtype=F32),
        vmem(HEADS, PATCHES, PATCHES, dtype=F32),
        *[vmem(PATCHES, PAD, dtype=F32) for _ in range(3)],
        vmem(HALF, D, dtype=F32),
        dma((10,)),
        dma((2, 3)), dma((2, 3)),
        dma((2, 4)), dma((2, 4)),
        dma((1,)), dma((1,)),
        *[dma((SEQ,)) for _ in range(8)],
        dma((4,)), dma((4,)),
        dma((2, 4)), dma((2, 4)),
        dma((2, 4)), dma((2, 4)),
        dma((2,)), dma((2, 4)),
        dma((2, 4)), dma((2, 4)),
        dma((2, 4)), dma((2,)),
    ]
    hbm = pl.BlockSpec(memory_space=pl.ANY)
    spatial, temporal, rows = pl.pallas_call(
        kernel,
        name="attention_backward",
        out_shape=[
            jax.ShapeDtypeStruct((PATCHES, WIDTH), BF16),
            jax.ShapeDtypeStruct((FRAMES, GROUP, WIDTH), BF16),
            jax.ShapeDtypeStruct((2, ROWS, D), BF16),
        ],
        in_specs=[hbm] * 4,
        out_specs=[hbm] * 3,
        scratch_shapes=scratch,
        compiler_params=pltpu.CompilerParams(
            collective_id=0, has_side_effects=True, vmem_limit_bytes=56 * 2**20
        ),
    )(
        qkv_spatial,
        qkv_temporal.reshape(FRAMES, GROUP, WIDTH),
        out_grad,
        jnp.transpose(out_proj, (1, 0, 2)),
    )
    return spatial, temporal.reshape(PATCHES, WIDTH), jnp.transpose(rows, (1, 0, 2))


def solution(mesh):
    placed = (
        P(("rep", "seq"), None),
        P(("rep", "seq"), None),
        P(("rep", "seq"), None),
        P("seq", None, None),
    )
    return jax.shard_map(
        per_device,
        mesh=mesh,
        in_specs=placed,
        out_specs=(P(("rep", "seq"), None), P(("rep", "seq"), None), P("seq", None, None)),
        check_vma=False,
    )
```

time: 530 us -> 130 us (0.25)
  the two profiles are of different devices: /device:TPU:2 before, /device:TPU:16 now
where the time goes in v1:
time: 130 us
  Pallas kernels  120 us (92%)
  local copies, waits for them, and re-layouts  9.46 us (7%)
    pallas_call x1, Pallas kernels, per_device(): pl.pallas_call(kernel, name='attention_backward', out_shape=[jax.ShapeDty...  120 us
    unnamed x12, local copies, waits for them, and re-layouts  9.46 us

profile of v1, /device:TPU:16, one launch (start us, length us, event | category | flops | bytes accessed | tf_op | source)
XLA Modules:
  0.0 130.2 jit_solution(5679370195827306640)
XLA Ops:
  0.6 1.5 %copy.14 = bf16[18,2,1152]{2,0,1:T(8,128)(2,1)} copy(bf16[18,2,1152]{2,1,0:T(2,128)(2,1)} %param.7) | data formatting | bytes 165888 | tf_op args[3]
  2.2 0.0 copy-start.1
  2.2 2.3 %copy.9.qkvs_ref = bf16[256,1728]{1,0:T(8,128)(2,1)} copy(bf16[256,1728]{0,1:T(8,128)(2,1)} %param.4) | data formatting | bytes 1769472 | tf_op args[0]
  4.5 0.0 copy-done.1
  4.5 1.4 %copy.7 = bf16[256,1728]{1,0:T(8,128)(2,1)} copy(bf16[256,1728]{0,1:T(8,128)(2,1)S(1)} %copy-done.1) | data formatting | bytes 1769472 | tf_op args[1]
  5.8 120.1 %attention_backward.1 = (bf16[256,1728]{1,0:T(8,128)(2,1)}, bf16[32,8,1728]{2,1,0:T(8,128)(2,1)}, bf16[2,18,1152]{2,1,0:T(8,128)(2,1)}) custom-call(bf16[256,1728]{1,0:T(8,128)(2,1)} %copy.9.qkvs_ref, bf16[32,8,1728]{2,1,0:T(8,128)(2,1)} %bitcast.6, bf16[256,1152]{1,0:T(8,128)(2,1)} %og_ref.1, bf16[2,18,1152]{2,1,0:T(8,128)(2,1)} %bitcast.8), custom_call_target="tpu_custom_call" | custom-call | tf_op jit(solution)/shard_map/attention_backward/pallas_call | solution.py:495
  125.9 0.0 copy-start
  125.9 2.3 %copy.10 = bf16[256,1728]{0,1:T(8,128)(2,1)} copy(bf16[256,1728]{1,0:T(8,128)(2,1)} %get-tuple-element.9) | data formatting | bytes 1769472
  128.2 0.0 copy-done
  128.2 0.0 copy-start.2
  128.2 1.3 copy.11
  129.5 0.0 copy-done.2
  129.5 0.7 copy.12
Async XLA Ops:
  2.2 2.3 %copy-start.1 = (bf16[256,1728]{0,1:T(8,128)(2,1)S(1)}, bf16[256,1728]{0,1:T(8,128)(2,1)}, u32[]{:S(2)}) copy-start(bf16[256,1728]{0,1:T(8,128)(2,1)} %param.5) | copy-start | bytes 2654212
  125.9 2.3 %copy-start = (bf16[32,8,1728]{2,1,0:T(8,128)(2,1)S(1)}, bf16[32,8,1728]{2,1,0:T(8,128)(2,1)}, u32[]{:S(2)}) copy-start(bf16[32,8,1728]{2,1,0:T(8,128)(2,1)} %get-tuple-element.7) | copy-start | bytes 2654212
  128.2 1.3 copy-start.2

commit v2 on v0

v2 whole, which is shorter than its diff:
```python
import functools

import jax
import jax.numpy as jnp
from jax import lax
from jax.experimental import pallas as pl
from jax.experimental.pallas import tpu as pltpu
from jax.sharding import PartitionSpec as P

HEADS, HEAD_DIM, PATCHES, FRAMES = 8, 72, 256, 32
INNER, WIDTH, D = 576, 1728, 1152
PART = 4
PAD = 384
FIELDS = 896
GROUP = 8
ROWS = 18
BLOCK = 24
PAIR = 40
QUAD = 4 * ROWS
HALF = 4 * QUAD
SEQ, TOKENS = 32, 131072
SCALING = HEAD_DIM**-0.5
FACTOR = float(TOKENS) ** -0.5
F32, BF16 = jnp.float32, jnp.bfloat16


def dot(left, right, dims=((1,), (0,))):
    return lax.dot_general(left, right, (dims, ((), ())), preferred_element_type=F32)


def kernel(
    qkvs_ref, qkvt_ref, og_ref, w_ref,
    gs_ref, gt_ref, gw_ref,
    qkvs, gsb, og2, qtin, qts, qtr, ogr, ogt, gts, gtr, gto, wraw, wz, wx, wmat, selw, selg, m2,
    gbuf, yrecv, ysum, xbuf, xrecv, zbuf, zrecv, z2buf, z2recv, res,
    qt, kt, vt, dt, probs_s, probs_t, acc0, acc1, acc2, mixs, dms, turn,
    lsem, wz_s, wz_r, wx_s, wx_r, ww_s, ww_r, og_s, og_r, a_s, a_r, b_s, b_r, d_s, d_r,
    p_s, p_r, y_s, y_r, x_s, x_r, z_s, z_r, zz_s, zz_r, f_s, f_r,
):
    rep, me = lax.axis_index("rep"), lax.axis_index("seq")
    zh, y = rep // 4, lax.rem(rep, 4)
    zl, x, core = me // 8, lax.rem(me // 2, 4), lax.rem(me, 2)
    z = 4 * zh + zl

    def at(rep_to, seq_to):
        return {"device_id": (rep_to, seq_to), "device_id_type": pl.DeviceIdType.MESH}

    def at_z(step):
        to = lax.rem(z + step + 16, 16)
        return at((to // 4) * 4 + y, lax.rem(to, 4) * 8 + lax.rem(me, 8))

    def at_y(step):
        return at(zh * 4 + lax.rem(y + step, 4), me)

    def at_zh(step):
        return at(lax.rem(zh + step, 4) * 4 + y, me)

    def at_x(step):
        return at(rep, zl * 8 + lax.rem(x + step, 4) * 2 + core)

    partner = at(rep, me + 1 - 2 * core)

    def remote(src, dst, send, recv, target):
        return pltpu.make_async_remote_copy(
            src_ref=src, dst_ref=dst, send_sem=send, recv_sem=recv, **target
        )

    barrier = pltpu.get_barrier_semaphore()

    def greet(k, carry):
        pl.semaphore_signal(barrier, inc=1, **at(rep, lax.rem(me + k, SEQ)))
        return carry

    lax.fori_loop(1, SEQ, greet, 0)
    for step in (-1, -2, 1):
        pl.semaphore_signal(barrier, inc=1, **at_z(step))
    for step in (1, 2, 3):
        pl.semaphore_signal(barrier, inc=1, **at_y(step))
        pl.semaphore_signal(barrier, inc=1, **at_zh(step))

    local = [
        pltpu.make_async_copy(w_ref, wraw, lsem.at[0]),
        pltpu.make_async_copy(qkvs_ref, qkvs, lsem.at[1]),
        pltpu.make_async_copy(og_ref, og2.at[0], lsem.at[2]),
        pltpu.make_async_copy(qkvt_ref, qtin, lsem.at[3]),
        pltpu.make_async_copy(og_ref.at[me], ogr.at[0, me], lsem.at[5]),
    ]
    for copy in local:
        copy.start()
    local[0].wait()
    own_rows = wraw[...].astype(F32)
    for b in (0, 1):
        wz[b, zl] = jnp.concatenate(
            [own_rows[:, b, :], jnp.zeros((BLOCK - ROWS, D), F32)], axis=0
        ).astype(BF16)

    def units(half):
        return [
            (HEAD_DIM * (PART * w + i), HEADS * w + 2 * i + half) for w in range(3) for i in range(PART)
        ]

    local[3].wait()
    turn[3 * PART * HEAD_DIM :, :] = jnp.zeros((FIELDS - 3 * PART * HEAD_DIM, PATCHES), F32)
    own_fields = []

    def turn_fields(half):
        for row, field in units(half):
            turn[row : row + HEAD_DIM, :] = qtin[field].astype(F32)
        for first in range(0, FIELDS, 128):
            part = turn[first : first + 128, :].T.reshape(FRAMES, GROUP, 128)
            qts[half, :, :, first : first + 128] = part.astype(BF16)
        copy = pltpu.make_async_copy(qts.at[half, me], qtr.at[half, me], lsem.at[9 + half])
        copy.start()
        own_fields.append(copy)

    turn_fields(0)

    pl.semaphore_wait(barrier, 31 + 9)

    def rows_z(b):
        return [
            remote(wz.at[b, zl], wz.at[b, zl], wz_s.at[b, i], wz_r.at[b, i], at_z(step))
            for i, step in enumerate((1, 2, -1))
        ]

    along_z = [rows_z(b) for b in (0, 1)]
    for copy in along_z[1] + along_z[0]:
        copy.start()

    def exchange(src, dst, send, recv):
        def copy(k):
            to = lax.rem(me + k, SEQ)
            return remote(src.at[to], dst.at[me], send.at[k], recv.at[k], at(rep, to))

        def start(k, carry):
            copy(k).start()
            return carry

        def landed(k, carry):
            copy(k).wait_recv()
            return carry

        def sent(k, carry):
            copy(k).wait_send()
            return carry

        return (
            lambda: lax.fori_loop(1, SEQ, start, 0),
            lambda: lax.fori_loop(1, SEQ, landed, 0),
            lambda: lax.fori_loop(1, SEQ, sent, 0),
        )

    fields_out = [
        exchange(qts.at[half], qtr.at[half], a_s.at[half], a_r.at[half]) for half in (0, 1)
    ]
    cotangent_out = exchange(og_ref, ogr.at[0], b_s, b_r)
    fields_back = [
        exchange(gts.at[half], gtr.at[half], d_s.at[half], d_r.at[half]) for half in (0, 1)
    ]
    fields_out[0][0]()
    cotangent_out[0]()
    turn_fields(1)
    fields_out[1][0]()
    og_copy = remote(og2.at[0], og2.at[1], og_s.at[0], og_r.at[0], partner)
    local[2].wait()
    og_copy.start()

    r = lax.broadcasted_iota(jnp.int32, (HALF, 1), 0)
    block = (r * 3641) >> 16
    high, low, j = block >> 2, block & 3, r - ROWS * block
    n = lax.broadcasted_iota(jnp.int32, (HALF, PAD), 1)
    for which in (0, 1):
        parity = core if which == 0 else 1 - core
        own = ROWS * (8 * low + 2 * high + parity) + j
        head = (own * 911) >> 16
        column = HEAD_DIM * (head >> 1) + own - HEAD_DIM * head
        for half in (0, 1):
            hit = (n == column) & ((head & 1) == half)
            selw[half, HALF * which : HALF * (which + 1), :] = jnp.where(hit, 1.0, 0.0).astype(BF16)
    r = lax.broadcasted_iota(jnp.int32, (4 * PAIR, 1), 0)
    n = lax.broadcasted_iota(jnp.int32, (4 * PAIR, PAD), 1)
    high = (r * 1639) >> 16
    low = jnp.where(r - PAIR * high >= ROWS, 1, 0)
    j = r - PAIR * high - ROWS * low
    for which in (0, 1):
        parity = core if which == 0 else 1 - core
        hit = (n == HEAD_DIM * high + ROWS * (2 * low + parity) + j) & (j < ROWS)
        selg[which] = jnp.where(hit, 1.0, 0.0).astype(BF16)
    mixs[...] = jnp.zeros_like(mixs)

    def split(half):
        fields = qtr[half].astype(F32).reshape(PATCHES, FIELDS)
        qt[half] = fields[:, 0:PAD].astype(BF16)
        kt[half] = pltpu.roll(fields[:, 256:640], PAD - 32, 1).astype(BF16)
        vt[half] = pltpu.roll(fields[:, 512:FIELDS], PAD - 64, 1).astype(BF16)

    def window(h):
        first = (HEAD_DIM * h) // 128
        lane = lax.broadcasted_iota(jnp.int32, (1, 256), 1) + first * 128 - HEAD_DIM * h
        keep = jnp.where((lane >= 0) & (lane < HEAD_DIM), 1.0, 0.0).astype(BF16)
        return pl.ds(pl.multiple_of(first * 128, 128), 256), keep

    def forward(half):
        q, k, v = qt.at[half], kt.at[half], vt.at[half]
        acc0[...] = jnp.zeros_like(acc0)

        def head(h, carry):
            cols, keep = window(h)
            scores = dot(q[:, cols], k[:, cols] * keep, ((1,), (1,))) * SCALING
            a = lax.broadcasted_iota(jnp.int32, scores.shape, 0)
            b = lax.broadcasted_iota(jnp.int32, scores.shape, 1)
            scores = jnp.where(((a ^ b) & (GROUP - 1)) == 0, scores, -1e30)
            weights = jnp.exp(scores - jnp.max(scores, axis=1, keepdims=True))
            p = weights / jnp.sum(weights, axis=1, keepdims=True)
            probs_t[PART * half + h] = p
            acc0[:, cols] += dot(p.astype(BF16), v[:, cols] * keep)
            return carry

        lax.fori_loop(0, PART, head, 0, unroll=2)

    def backward(half):
        q, k, v, dm = qt.at[half], kt.at[half], vt.at[half], dt.at[half]
        for out in (acc0, acc1, acc2):
            out[...] = jnp.zeros_like(out)

        def head(h, carry):
            cols, keep = window(h)
            p = probs_t[PART * half + h]
            dm_h = dm[:, cols] * keep
            acc2[:, cols] += dot(p.astype(BF16), dm_h, ((0,), (0,)))
            dp = dot(dm_h, v[:, cols], ((1,), (1,)))
            dsc = (p * (dp - jnp.sum(dp * p, axis=1, keepdims=True))).astype(BF16)
            acc0[:, cols] += dot(dsc, k[:, cols] * keep)
            acc1[:, cols] += dot(dsc, q[:, cols] * keep, ((0,), (0,)))
            return carry

        lax.fori_loop(0, PART, head, 0, unroll=2)
        a = acc0[...] * SCALING
        b = pltpu.roll(acc1[...] * SCALING, 32, 1)
        c = pltpu.roll(acc2[...], 64, 1)

        def put(low, value):
            high = low + value.shape[1]
            gts[half, :, :, low:high] = value.reshape(FRAMES, GROUP, high - low).astype(BF16)

        put(0, a[:, 0:256])
        put(256, a[:, 256:PAD] + b[:, 0:128])
        put(384, b[:, 128:256])
        put(512, b[:, 256:PAD] + c[:, 0:128])
        put(640, c[:, 128:PAD])
        fields_back[half][0]()
        own[half].start()

    def forward_spatial(h, carry):
        scores = dot(qkvs[h], qkvs[HEADS + h], ((0,), (0,))) * SCALING
        weights = jnp.exp(scores - jnp.max(scores, axis=1, keepdims=True))
        p = weights / jnp.sum(weights, axis=1, keepdims=True)
        probs_s[h] = p
        rows = pl.ds(pl.multiple_of((h >> 1) * HEAD_DIM, 8), HEAD_DIM)
        mixs[h & 1, rows, :] = dot(qkvs[2 * HEADS + h], p.astype(BF16), ((1,), (1,)))
        return carry

    def backward_spatial(h, carry):
        p = probs_s[h]
        rows = pl.ds(pl.multiple_of((h >> 1) * HEAD_DIM, 8), HEAD_DIM)
        dm_h = dms[h & 1, rows, :].astype(BF16)
        dv = dot(dm_h, p.astype(BF16))
        dp = dot(dm_h, qkvs[2 * HEADS + h], ((0,), (0,)))
        dsc = (p * (dp - jnp.sum(dp * p, axis=1, keepdims=True))).astype(BF16)
        dq = dot(qkvs[HEADS + h], dsc, ((1,), (1,))) * SCALING
        dk = dot(qkvs[h], dsc) * SCALING
        gsb[h] = dq.astype(BF16)
        gsb[HEADS + h] = dk.astype(BF16)
        gsb[2 * HEADS + h] = dv.astype(BF16)
        return carry

    def rows_x(b):
        return [
            remote(
                wx.at[0, b, x], wx.at[0, b, x], wx_s.at[b, step], wx_r.at[b, step], at_x(step)
            )
            for step in (1, 2, 3)
        ]

    along_x = [rows_x(b) for b in (0, 1)]

    def rows_x_start(b):
        for copy in along_z[b]:
            copy.wait_recv()
        parts = [wz[b, i].astype(F32)[0:ROWS] for i in range(4)]
        wx[0, b, x] = jnp.concatenate(parts, axis=0).astype(BF16)
        for copy in along_x[b]:
            copy.start()

    to_partner = [
        remote(wx.at[0, b], wx.at[1, b], ww_s.at[b], ww_r.at[b], partner) for b in (0, 1)
    ]

    def rows_swap(b):
        for copy in along_x[b]:
            copy.wait_recv()
        to_partner[b].start()

    def rows_all(b):
        to_partner[b].wait_recv()
        for which in (0, 1):
            half = wx[which, b].astype(F32).reshape(HALF, D).astype(BF16)
            wmat[HALF * which : HALF * (which + 1), :] = half

    local[1].wait()
    lax.fori_loop(0, HEADS, forward_spatial, 0, unroll=2)

    def mixed_start(u, mixed, dims):
        m2[u, 0] = dot(selg[0], mixed, dims).astype(BF16)
        m2[u, 1] = dot(selg[1], mixed, dims).astype(BF16)
        copy = remote(m2.at[u, 1], m2.at[u, 2], p_s.at[u], p_r.at[u], partner)
        copy.start()
        return copy

    def flat(rows):
        return rows.astype(F32).reshape(PATCHES, D).astype(BF16)

    def along(u):
        return [
            remote(
                gbuf.at[u, (y + step) & 3], yrecv.at[u, step],
                y_s.at[u, step], y_r.at[u, step], at_y(step),
            )
            for step in (1, 2, 3)
        ]

    def reduce_y_start(u, cotangents):
        share = dot(m2[u, 0], cotangents[0]) + dot(m2[u, 2], cotangents[1])
        gbuf[u] = (share * FACTOR).reshape(4, PAIR, D).astype(BF16)
        for copy in along(u):
            copy.start()

    def send_x(u, i):
        to = 2 * (u & 1) + i
        return to, remote(
            xbuf.at[u, i], xrecv.at[u, (x - to) & 3],
            x_s.at[u, i], x_r.at[u, (x - to) & 3], at(rep, zl * 8 + to * 2 + core),
        )

    def reduce_x_start(u):
        for copy in along(u):
            copy.wait()
        total = gbuf[u, y].astype(F32)
        for step in (1, 2, 3):
            total += yrecv[u, step].astype(F32)
        ysum[...] = total
        for i in (0, 1):
            rows = ysum[ROWS * i : ROWS * (i + 1), :]
            xbuf[u, i] = jnp.concatenate(
                [rows, jnp.zeros((BLOCK - ROWS, D), F32)], axis=0
            ).astype(BF16)
            to, copy = send_x(u, i)
            pl.when(x != to)(copy.start)

    def reduce_x_end(u):
        for i in (0, 1):
            to, copy = send_x(u, i)
            pl.when(x != to)(copy.wait_send)

    def here(u):
        return (x >> 1) == (u & 1)

    def reduce_z_start(u):
        b = u >> 1

        @pl.when(here(u))
        def _():
            total = xbuf[u, x & 1].astype(F32)
            for step in (1, 2, 3):
                arrived = xrecv.at[u, step]
                remote(arrived, arrived, x_s.at[u, 0], x_r.at[u, step], partner).wait_recv()
                total += xrecv[u, step].astype(F32)
            zbuf[b] = total.astype(BF16)
            pl.when(zl != y)(gather_z(b, 0).start)

    def gather_z(b, step):
        slot = lax.rem(zl - y + 4, 4) if step == 0 else step
        return remote(
            zbuf.at[b], zrecv.at[b, slot], z_s.at[b], z_r.at[b, slot],
            at(rep, y * 8 + lax.rem(me, 8)),
        )

    def spread_zh(b):
        return [
            remote(
                z2buf.at[b], z2recv.at[b, step], zz_s.at[b, step], zz_r.at[b, step], at_zh(step)
            )
            for step in (1, 2, 3)
        ]

    def reduce_zh_start(u):
        b = u >> 1

        @pl.when(here(u))
        def _stage():
            @pl.when(zl != y)
            def _():
                gather_z(b, 0).wait_send()

            @pl.when(zl == y)
            def _():
                total = zbuf[b].astype(F32)
                for step in (1, 2, 3):
                    gather_z(b, step).wait_recv()
                    total += zrecv[b, step].astype(F32)
                z2buf[b] = total.astype(BF16)
                for copy in spread_zh(b):
                    copy.start()

    def spread_y(b):
        return [
            remote(res.at[b], res.at[b], f_s.at[b, step], f_r.at[b], at_y(step))
            for step in (1, 2, 3)
        ]

    def spread_start(u):
        b = u >> 1

        @pl.when(here(u))
        def _stage():
            @pl.when(zl == y)
            def _():
                total = z2buf[b].astype(F32)
                for step, copy in zip((1, 2, 3), spread_zh(b), strict=True):
                    copy.wait()
                    total += z2recv[b, step].astype(F32)
                res[b] = total.astype(BF16)
                for copy in spread_y(b):
                    copy.start()

    def spread_end(u):
        b = u >> 1

        @pl.when(here(u))
        def _stage():
            @pl.when(zl == y)
            def _():
                for copy in spread_y(b):
                    copy.wait_send()

            @pl.when(zl != y)
            def _():
                spread_y(b)[0].wait_recv()

    swap_s = [mixed_start(half, mixs[half].astype(BF16), ((1,), (0,))) for half in (0, 1)]
    rows_x_start(1)
    own = [
        pltpu.make_async_copy(gts.at[0, me], gtr.at[0, me], lsem.at[4]),
        pltpu.make_async_copy(gts.at[1, me], gtr.at[1, me], lsem.at[6]),
        pltpu.make_async_copy(gsb, gs_ref, lsem.at[7]),
        pltpu.make_async_copy(gto, gt_ref, lsem.at[8]),
        pltpu.make_async_copy(res, gw_ref, lsem.at[11]),
    ]
    og_copy.wait()
    ogt[0] = flat(og2[0])
    ogt[1] = flat(og2[1])
    for half in (0, 1):
        swap_s[half].wait()
        reduce_y_start(half, (ogt[0], ogt[1]))
    rows_swap(1)

    def forward_half(half):
        own_fields[half].wait()
        fields_out[half][1]()
        split(half)
        forward(half)
        return mixed_start(2 + half, acc0[...].astype(BF16), ((1,), (1,)))

    for half in (0, 1):
        reduce_x_start(half)
    swap_t = forward_half(0)
    for half in (0, 1):
        reduce_z_start(half)
    rows_all(1)
    rows_x_start(0)

    local[4].wait()
    cotangent_out[1]()
    ogr_copy = remote(ogr.at[0], ogr.at[1], og_s.at[1], og_r.at[1], partner)
    ogr_copy.start()
    ogt[0] = flat(ogr[0])
    dah = dot(ogt[0], wmat[...], ((1,), (1,))).astype(BF16)
    for half in (0, 1):
        dt[half] = dot(dah, selw[half]).astype(BF16)
    swap_t.wait()
    ogr_copy.wait()
    ogt[1] = flat(ogr[1])
    reduce_y_start(2, (ogt[0], ogt[1]))
    for half in (0, 1):
        reduce_zh_start(half)
    rows_swap(0)
    backward(0)
    reduce_x_start(2)

    swap_t = forward_half(1)
    reduce_z_start(2)
    swap_t.wait()
    reduce_y_start(3, (ogt[0], ogt[1]))
    backward(1)
    reduce_x_start(3)
    reduce_z_start(3)
    for half in (0, 1):
        spread_start(half)
    reduce_zh_start(2)

    def turn_back(half):
        own[half].wait()
        fields_back[half][1]()
        for first in range(0, FIELDS, 128):
            part = gtr[half, :, :, first : first + 128].astype(F32)
            turn[first : first + 128, :] = part.reshape(PATCHES, 128).T
        for row, field in units(half):
            gto[field] = turn[row : row + HEAD_DIM, :].astype(BF16)
    turn_back(0)
    reduce_zh_start(3)
    spread_start(2)

    rows_all(0)
    dah = dot(wmat[...], flat(og2[0]), ((1,), (1,))).astype(BF16)
    for half in (0, 1):
        dms[half] = dot(selw[half], dah, ((0,), (0,)))
    lax.fori_loop(0, HEADS, backward_spatial, 0, unroll=2)
    own[2].start()

    spread_start(3)
    turn_back(1)
    own[3].start()
    for u in range(4):
        spread_end(u)
    own[4].start()

    for copy in [c for b in (0, 1) for c in along_z[b] + along_x[b] + [to_partner[b]]]:
        copy.wait_send()
    for u in range(4):
        reduce_x_end(u)
    cotangent_out[2]()
    for half in (0, 1):
        fields_out[half][2]()
        fields_back[half][2]()
    for copy in own[2:]:
        copy.wait()


def finish(gs_ref, gt_ref, rows_ref, gs_out, gt_out, rows_out, fields, rows, sems):
    load = [pltpu.make_async_copy(rows_ref, rows, sems.at[0])]
    store = []
    for i, (src, dst) in enumerate(((gs_ref, gs_out), (gt_ref, gt_out))):
        for w in range(3):
            part, k = pl.ds(HEADS * w, HEADS), 3 * i + w
            load.append(pltpu.make_async_copy(src.at[part], fields.at[k], sems.at[1 + k]))
            store.append(pltpu.make_async_copy(fields.at[k], dst.at[part], sems.at[7 + k]))
    for copy in load:
        copy.start()
    load[0].wait()
    both = [rows[b].astype(F32)[0:ROWS] for b in (0, 1)]
    rows_out[...] = jnp.stack(both, axis=1).astype(BF16)
    for arrived, copy in zip(load[1:], store, strict=True):
        arrived.wait()
        copy.start()
    for copy in store:
        copy.wait()


def per_device(qkv_spatial, qkv_temporal, out_grad, out_proj):
    def vmem(*shape, dtype=BF16):
        return pltpu.VMEM(shape, dtype)

    dma = pltpu.SemaphoreType.DMA
    scratch = [
        vmem(3 * HEADS, HEAD_DIM, PATCHES),
        vmem(3 * HEADS, HEAD_DIM, PATCHES),
        vmem(2, FRAMES, GROUP, D),
        vmem(3 * HEADS, HEAD_DIM, PATCHES),
        vmem(2, FRAMES, GROUP, FIELDS),
        vmem(2, FRAMES, GROUP, FIELDS),
        vmem(2, FRAMES, GROUP, D),
        vmem(2, PATCHES, D),
        vmem(2, FRAMES, GROUP, FIELDS),
        vmem(2, FRAMES, GROUP, FIELDS),
        vmem(3 * HEADS, HEAD_DIM, PATCHES),
        vmem(ROWS, 2, D),
        vmem(2, 4, BLOCK, D),
        vmem(2, 2, 4, QUAD, D),
        vmem(INNER, D),
        vmem(2, INNER, PAD),
        vmem(2, 4 * PAIR, PAD),
        vmem(4, 3, 4 * PAIR, PATCHES),
        vmem(4, 4, PAIR, D),
        vmem(4, 4, PAIR, D),
        vmem(PAIR, D, dtype=F32),
        vmem(4, 2, BLOCK, D),
        vmem(4, 4, BLOCK, D),
        vmem(2, BLOCK, D),
        vmem(2, 4, BLOCK, D),
        vmem(2, BLOCK, D),
        vmem(2, 4, BLOCK, D),
        vmem(2, BLOCK, D),
        *[vmem(2, PATCHES, PAD) for _ in range(4)],
        vmem(HEADS, PATCHES, PATCHES, dtype=F32),
        vmem(HEADS, PATCHES, PATCHES, dtype=F32),
        *[vmem(PATCHES, PAD, dtype=F32) for _ in range(3)],
        *[vmem(2, PAD, PATCHES, dtype=F32) for _ in range(2)],
        vmem(FIELDS, PATCHES, dtype=F32),
        dma((12,)),
        dma((2, 3)), dma((2, 3)),
        dma((2, 4)), dma((2, 4)),
        dma((2,)), dma((2,)),
        dma((2,)), dma((2,)),
        dma((2, SEQ)), dma((2, SEQ)),
        dma((SEQ,)), dma((SEQ,)),
        dma((2, SEQ)), dma((2, SEQ)),
        dma((4,)), dma((4,)),
        dma((4, 4)), dma((4, 4)),
        dma((4, 2)), dma((4, 4)),
        dma((2,)), dma((2, 4)),
        dma((2, 4)), dma((2, 4)),
        dma((2, 4)), dma((2,)),
    ]
    hbm = pl.BlockSpec(memory_space=pl.ANY)
    spatial, temporal, rows = pl.pallas_call(
        kernel,
        name="attention_backward",
        out_shape=[
            jax.ShapeDtypeStruct((3 * HEADS, HEAD_DIM, PATCHES), BF16),
            jax.ShapeDtypeStruct((3 * HEADS, HEAD_DIM, PATCHES), BF16),
            jax.ShapeDtypeStruct((2, BLOCK, D), BF16),
        ],
        in_specs=[hbm] * 4,
        out_specs=[hbm] * 3,
        scratch_shapes=scratch,
        compiler_params=pltpu.CompilerParams(
            collective_id=0, has_side_effects=True, vmem_limit_bytes=56 * 2**20
        ),
    )(
        qkv_spatial.T.reshape(3 * HEADS, HEAD_DIM, PATCHES),
        qkv_temporal.T.reshape(3 * HEADS, HEAD_DIM, PATCHES),
        out_grad.reshape(FRAMES, GROUP, D),
        out_proj,
    )
    spatial, temporal, rows = pl.pallas_call(
        finish,
        name="finish",
        out_shape=[
            jax.ShapeDtypeStruct((3 * HEADS, HEAD_DIM, PATCHES), BF16),
            jax.ShapeDtypeStruct((3 * HEADS, HEAD_DIM, PATCHES), BF16),
            jax.ShapeDtypeStruct((ROWS, 2, D), BF16),
        ],
        in_specs=[hbm] * 3,
        out_specs=[hbm, hbm, pl.BlockSpec(memory_space=pltpu.VMEM)],
        scratch_shapes=[vmem(6, HEADS, HEAD_DIM, PATCHES), vmem(2, BLOCK, D), dma((13,))],
        compiler_params=pltpu.CompilerParams(vmem_limit_bytes=56 * 2**20),
    )(spatial, temporal, rows)
    return spatial.reshape(WIDTH, PATCHES).T, temporal.reshape(WIDTH, PATCHES).T, rows


def solution(mesh):
    placed = (
        P(("rep", "seq"), None),
        P(("rep", "seq"), None),
        P(("rep", "seq"), None),
        P("seq", None, None),
    )
    return jax.shard_map(
        per_device,
        mesh=mesh,
        in_specs=placed,
        out_specs=(P(("rep", "seq"), None), P(("rep", "seq"), None), P("seq", None, None)),
        check_vma=False,
    )
```

time: 530 us -> 108 us (0.20)
  the two profiles are of different devices: /device:TPU:2 before, /device:TPU:22 now
where the time goes in v2:
time: 108 us; the launch traced here: 107 us
  Pallas kernels  107 us (99%)
    pallas_call x1, Pallas kernels, per_device(): pl.pallas_call(kernel, name='attention_backward', out_shape=[jax.ShapeDty...  104 us
    pallas_call x1, Pallas kernels, per_device(): pl.pallas_call(finish, name='finish', out_shape=[jax.ShapeDtypeStruct((3...  2.99 us

profile of v2, /device:TPU:22, one launch (start us, length us, event | category | flops | bytes accessed | tf_op | source)
XLA Modules:
  0.0 107.4 jit_solution(8415997115962158961)
XLA Ops:
  0.6 103.8 %attention_backward.1 = (bf16[24,72,256]{2,1,0:T(8,128)(2,1)}, bf16[24,72,256]{2,1,0:T(8,128)(2,1)}, bf16[2,24,1152]{2,1,0:T(8,128)(2,1)}) custom-call(bf16[24,72,256]{2,1,0:T(8,128)(2,1)} %bitcast.13, bf16[24,72,256]{2,1,0:T(8,128)(2,1)} %bitcast.14, bf16[32,8,1152]{2,1,0:T(8,128)(2,1)} %bitcast.15, bf16[18,2,1152]{2,1,0:T(2,128)(2,1)} %w_ref.1), custom_call_target="tpu_custom_call" | custom-call | tf_op jit(solution)/shard_map/attention_backward/pallas_call | solution.py:625
  104.4 3.0 %finish.1 = (bf16[24,72,256]{2,1,0:T(8,128)(2,1)}, bf16[24,72,256]{2,1,0:T(8,128)(2,1)}, bf16[18,2,1152]{2,1,0:T(2,128)(2,1)}) custom-call(bf16[24,72,256]{2,1,0:T(8,128)(2,1)} %get-tuple-element.9.gs_ref, bf16[24,72,256]{2,1,0:T(8,128)(2,1)} %get-tuple-element.10.gt_ref, bf16[2,24,1152]{2,1,0:T(8,128)(2,1)} %get-tuple-element.11.rows_ref), custom_call_target="tpu_custom_call" | custom-call | tf_op jit(solution)/shard_map/finish/pallas_call | solution.py:645

commit v3 on v2

--- a/solution.py
+++ b/solution.py
@@ -31,10 +31,10 @@
 def kernel(
     qkvs_ref, qkvt_ref, og_ref, w_ref,
     gs_ref, gt_ref, gw_ref,
-    qkvs, gsb, og2, qtin, qts, qtr, ogr, ogt, gts, gtr, gto, wraw, wz, wx, wmat, selw, selg, m2,
+    qkvs, gsb, og2, qtin, qts, qtr, ogr, ogt, gts, gtr, gto, wraw, wown, wz, wx, wmat, selw, selg, m2,
     gbuf, yrecv, ysum, xbuf, xrecv, zbuf, zrecv, z2buf, z2recv, res,
     qt, kt, vt, dt, probs_s, probs_t, acc0, acc1, acc2, mixs, dms, turn,
-    lsem, wz_s, wz_r, wx_s, wx_r, ww_s, ww_r, og_s, og_r, a_s, a_r, b_s, b_r, d_s, d_r,
+    lsem, wz_s, wz_r, wy_s, wy_r, wx_s, wx_r, ww_s, ww_r, og_s, og_r, a_s, a_r, b_s, b_r, d_s, d_r,
     p_s, p_r, y_s, y_r, x_s, x_r, z_s, z_r, zz_s, zz_r, f_s, f_r,
 ):
     rep, me = lax.axis_index("rep"), lax.axis_index("seq")
@@ -89,10 +89,13 @@
         copy.start()
     local[0].wait()
     own_rows = wraw[...].astype(F32)
-    for b in (0, 1):
-        wz[b, zl] = jnp.concatenate(
-            [own_rows[:, b, :], jnp.zeros((BLOCK - ROWS, D), F32)], axis=0
-        ).astype(BF16)
+    rest = jnp.zeros((PAIR - 2 * ROWS, D), F32)
+    own_rows = jnp.concatenate([own_rows[:, 0, :], own_rows[:, 1, :], rest], axis=0)
+    wown[...] = own_rows.astype(BF16)
+
+    @pl.when(zl == y)
+    def _():
+        wz[y] = wown[...]
 
     def units(half):
         return [
@@ -117,15 +120,19 @@
 
     pl.semaphore_wait(barrier, 31 + 9)
 
-    def rows_z(b):
-        return [
-            remote(wz.at[b, zl], wz.at[b, zl], wz_s.at[b, i], wz_r.at[b, i], at_z(step))
-            for i, step in enumerate((1, 2, -1))
-        ]
-
-    along_z = [rows_z(b) for b in (0, 1)]
-    for copy in along_z[1] + along_z[0]:
-        copy.start()
+    along_z = [
+        remote(wown, wz.at[y], wz_s.at[i], wz_r.at[0], at_z(step))
+        for i, step in enumerate((1, 2, -1))
+    ]
+    along_y = [
+        remote(wz.at[y], wz.at[y], wy_s.at[step], wy_r.at[step], at_y(step))
+        for step in (1, 2, 3)
+    ]
+
+    @pl.when(zl == y)
+    def _():
+        for copy in along_z + along_y:
+            copy.start()
 
     def exchange(src, dst, send, recv):
         def copy(k):
@@ -161,6 +168,13 @@
     cotangent_out[0]()
     turn_fields(1)
     fields_out[1][0]()
+
+    @pl.when(zl != y)
+    def _():
+        along_z[0].wait_recv()
+        for copy in along_y:
+            copy.start()
+
     og_copy = remote(og2.at[0], og2.at[1], og_s.at[0], og_r.at[0], partner)
     local[2].wait()
     og_copy.start()
@@ -216,7 +230,7 @@
             acc0[:, cols] += dot(p.astype(BF16), v[:, cols] * keep)
             return carry
 
-        lax.fori_loop(0, PART, head, 0, unroll=2)
+        lax.fori_loop(0, PART, head, 0, unroll=4)
 
     def backward(half):
         q, k, v, dm = qt.at[half], kt.at[half], vt.at[half], dt.at[half]
@@ -234,7 +248,7 @@
             acc1[:, cols] += dot(dsc, q[:, cols] * keep, ((0,), (0,)))
             return carry
 
-        lax.fori_loop(0, PART, head, 0, unroll=2)
+        lax.fori_loop(0, PART, head, 0, unroll=4)
         a = acc0[...] * SCALING
         b = pltpu.roll(acc1[...] * SCALING, 32, 1)
         c = pltpu.roll(acc2[...], 64, 1)
@@ -285,9 +299,7 @@
     along_x = [rows_x(b) for b in (0, 1)]
 
     def rows_x_start(b):
-        for copy in along_z[b]:
-            copy.wait_recv()
-        parts = [wz[b, i].astype(F32)[0:ROWS] for i in range(4)]
+        parts = [wz[i].astype(F32)[ROWS * b : ROWS * (b + 1)] for i in range(4)]
         wx[0, b, x] = jnp.concatenate(parts, axis=0).astype(BF16)
         for copy in along_x[b]:
             copy.start()
@@ -308,7 +320,7 @@
             wmat[HALF * which : HALF * (which + 1), :] = half
 
     local[1].wait()
-    lax.fori_loop(0, HEADS, forward_spatial, 0, unroll=2)
+    lax.fori_loop(0, HEADS, forward_spatial, 0, unroll=4)
 
     def mixed_start(u, mixed, dims):
         m2[u, 0] = dot(selg[0], mixed, dims).astype(BF16)
@@ -329,8 +341,10 @@
             for step in (1, 2, 3)
         ]
 
-    def reduce_y_start(u, cotangents):
-        share = dot(m2[u, 0], cotangents[0]) + dot(m2[u, 2], cotangents[1])
+    def reduce_y_start(u, cotangents, swap):
+        share = dot(m2[u, 0], cotangents[0])
+        swap.wait()
+        share += dot(m2[u, 2], cotangents[1])
         gbuf[u] = (share * FACTOR).reshape(4, PAIR, D).astype(BF16)
         for copy in along(u):
             copy.start()
@@ -448,6 +462,8 @@
                 spread_y(b)[0].wait_recv()
 
     swap_s = [mixed_start(half, mixs[half].astype(BF16), ((1,), (0,))) for half in (0, 1)]
+    for copy in along_y:
+        copy.wait_recv()
     rows_x_start(1)
     own = [
         pltpu.make_async_copy(gts.at[0, me], gtr.at[0, me], lsem.at[4]),
@@ -460,8 +476,7 @@
     ogt[0] = flat(og2[0])
     ogt[1] = flat(og2[1])
     for half in (0, 1):
-        swap_s[half].wait()
-        reduce_y_start(half, (ogt[0], ogt[1]))
+        reduce_y_start(half, (ogt[0], ogt[1]), swap_s[half])
     rows_swap(1)
 
     def forward_half(half):
@@ -487,10 +502,9 @@
     dah = dot(ogt[0], wmat[...], ((1,), (1,))).astype(BF16)
     for half in (0, 1):
         dt[half] = dot(dah, selw[half]).astype(BF16)
-    swap_t.wait()
     ogr_copy.wait()
     ogt[1] = flat(ogr[1])
-    reduce_y_start(2, (ogt[0], ogt[1]))
+    reduce_y_start(2, (ogt[0], ogt[1]), swap_t)
     for half in (0, 1):
         reduce_zh_start(half)
     rows_swap(0)
@@ -498,9 +512,8 @@
     reduce_x_start(2)
 
     swap_t = forward_half(1)
+    reduce_y_start(3, (ogt[0], ogt[1]), swap_t)
     reduce_z_start(2)
-    swap_t.wait()
-    reduce_y_start(3, (ogt[0], ogt[1]))
     backward(1)
     reduce_x_start(3)
     reduce_z_start(3)
@@ -516,8 +529,8 @@
             turn[first : first + 128, :] = part.reshape(PATCHES, 128).T
         for row, field in units(half):
             gto[field] = turn[row : row + HEAD_DIM, :].astype(BF16)
+    reduce_zh_start(3)
     turn_back(0)
-    reduce_zh_start(3)
     spread_start(2)
 
     rows_all(0)
@@ -534,8 +547,14 @@
         spread_end(u)
     own[4].start()
 
-    for copy in [c for b in (0, 1) for c in along_z[b] + along_x[b] + [to_partner[b]]]:
+    for copy in along_y + along_x[0] + along_x[1] + to_partner:
         copy.wait_send()
+
+    @pl.when(zl == y)
+    def _():
+        for copy in along_z:
+            copy.wait_send()
+
     for u in range(4):
         reduce_x_end(u)
     cotangent_out[2]()
@@ -584,7 +603,8 @@
         vmem(2, FRAMES, GROUP, FIELDS),
         vmem(3 * HEADS, HEAD_DIM, PATCHES),
         vmem(ROWS, 2, D),
-        vmem(2, 4, BLOCK, D),
+        vmem(PAIR, D),
+        vmem(4, PAIR, D),
         vmem(2, 2, 4, QUAD, D),
         vmem(INNER, D),
         vmem(2, INNER, PAD),
@@ -607,7 +627,8 @@
         *[vmem(2, PAD, PATCHES, dtype=F32) for _ in range(2)],
         vmem(FIELDS, PATCHES, dtype=F32),
         dma((12,)),
-        dma((2, 3)), dma((2, 3)),
+        dma((3,)), dma((1,)),
+        dma((4,)), dma((4,)),
         dma((2, 4)), dma((2, 4)),
         dma((2,)), dma((2,)),
         dma((2,)), dma((2,)),

time: 108 us -> 102 us (0.944)
  the two profiles are of different devices: /device:TPU:22 before, /device:TPU:70 now
where the time goes in v3:
time: 102 us
  Pallas kernels  101 us (99%)
    pallas_call x1, Pallas kernels, per_device(): pl.pallas_call(kernel, name='attention_backward', out_shape=[jax.ShapeDty...  98.2 us
    pallas_call x1, Pallas kernels, per_device(): pl.pallas_call(finish, name='finish', out_shape=[jax.ShapeDtypeStruct((3...  2.99 us

profile of v3, /device:TPU:70, one launch (start us, length us, event | category | flops | bytes accessed | tf_op | source)
XLA Modules:
  0.0 102.0 jit_solution(9392131110463731137)
XLA Ops:
  0.6 98.2 %attention_backward.1 = (bf16[24,72,256]{2,1,0:T(8,128)(2,1)}, bf16[24,72,256]{2,1,0:T(8,128)(2,1)}, bf16[2,24,1152]{2,1,0:T(8,128)(2,1)}) custom-call(bf16[24,72,256]{2,1,0:T(8,128)(2,1)} %bitcast.13, bf16[24,72,256]{2,1,0:T(8,128)(2,1)} %bitcast.14, bf16[32,8,1152]{2,1,0:T(8,128)(2,1)} %bitcast.15, bf16[18,2,1152]{2,1,0:T(2,128)(2,1)} %w_ref.1), custom_call_target="tpu_custom_call" | custom-call | tf_op jit(solution)/shard_map/attention_backward/pallas_call | solution.py:646
  98.8 3.0 %finish.1 = (bf16[24,72,256]{2,1,0:T(8,128)(2,1)}, bf16[24,72,256]{2,1,0:T(8,128)(2,1)}, bf16[18,2,1152]{2,1,0:T(2,128)(2,1)}) custom-call(bf16[24,72,256]{2,1,0:T(8,128)(2,1)} %get-tuple-element.9.gs_ref, bf16[24,72,256]{2,1,0:T(8,128)(2,1)} %get-tuple-element.10.gt_ref, bf16[2,24,1152]{2,1,0:T(8,128)(2,1)} %get-tuple-element.11.rows_ref), custom_call_target="tpu_custom_call" | custom-call | tf_op jit(solution)/shard_map/finish/pallas_call | solution.py:666

commit v4 on v3

--- a/solution.py
+++ b/solution.py
@@ -531,7 +531,6 @@
             gto[field] = turn[row : row + HEAD_DIM, :].astype(BF16)
     reduce_zh_start(3)
     turn_back(0)
-    spread_start(2)
 
     rows_all(0)
     dah = dot(wmat[...], flat(og2[0]), ((1,), (1,))).astype(BF16)
@@ -540,6 +539,7 @@
     lax.fori_loop(0, HEADS, backward_spatial, 0, unroll=2)
     own[2].start()
 
+    spread_start(2)
     spread_start(3)
     turn_back(1)
     own[3].start()

time: 102 us -> 102 us (level)
  no operation moved by 1% of the time
where the time goes in v4:
time: 102 us
  Pallas kernels  101 us (99%)
    pallas_call x1, Pallas kernels, per_device(): pl.pallas_call(kernel, name='attention_backward', out_shape=[jax.ShapeDty...  98.2 us
    pallas_call x1, Pallas kernels, per_device(): pl.pallas_call(finish, name='finish', out_shape=[jax.ShapeDtypeStruct((3...  2.99 us

profile of v4, /device:TPU:70, one launch (start us, length us, event | category | flops | bytes accessed | tf_op | source)
XLA Modules:
  0.0 102.0 jit_solution(1361224264607759457)
XLA Ops:
  0.6 98.2 %attention_backward.1 = (bf16[24,72,256]{2,1,0:T(8,128)(2,1)}, bf16[24,72,256]{2,1,0:T(8,128)(2,1)}, bf16[2,24,1152]{2,1,0:T(8,128)(2,1)}) custom-call(bf16[24,72,256]{2,1,0:T(8,128)(2,1)} %bitcast.13, bf16[24,72,256]{2,1,0:T(8,128)(2,1)} %bitcast.14, bf16[32,8,1152]{2,1,0:T(8,128)(2,1)} %bitcast.15, bf16[18,2,1152]{2,1,0:T(2,128)(2,1)} %w_ref.1), custom_call_target="tpu_custom_call" | custom-call | tf_op jit(solution)/shard_map/attention_backward/pallas_call | solution.py:646
  98.8 3.0 %finish.1 = (bf16[24,72,256]{2,1,0:T(8,128)(2,1)}, bf16[24,72,256]{2,1,0:T(8,128)(2,1)}, bf16[18,2,1152]{2,1,0:T(2,128)(2,1)}) custom-call(bf16[24,72,256]{2,1,0:T(8,128)(2,1)} %get-tuple-element.9.gs_ref, bf16[24,72,256]{2,1,0:T(8,128)(2,1)} %get-tuple-element.10.gt_ref, bf16[2,24,1152]{2,1,0:T(8,128)(2,1)} %get-tuple-element.11.rows_ref), custom_call_target="tpu_custom_call" | custom-call | tf_op jit(solution)/shard_map/finish/pallas_call | solution.py:666
